TPU v7x, 512 devices: a whole 4x4x16 slice. The times are simulated.
512 devices in a mesh: ctx: 16 (over z_lo, core), head: 32 (over z_hi, y, x).
Axes of the slice: x: 4, y: 4, z: 16 (z_hi: 2, z_lo: 8; z = z_hi * 8 + z_lo), core: 2. Of those that a mesh axis runs over, the one named last changes fastest.
Arguments:
- queries: bfloat16 [4096, 8192], P('ctx', 'head'), may hold values from -5 to 5
- key_rows: bfloat16 [4096, 1024], P('ctx'), may hold values from -5 to 5
- value_rows: bfloat16 [4096, 1024], P('ctx'), may hold values from -6 to 6
- state_input: bfloat16 [4096, 8192], P('ctx', 'head'), may hold values from -6 to 6
- state_write: bfloat16 [4096, 8192], P('ctx', 'head'), may hold values from -0.119628906 to 0.119628906
- state_read: bfloat16 [4096, 8192], P('ctx', 'head'), may hold values from -6 to 6
- gate_input: bfloat16 [4096, 8192], P('ctx', 'head'), may hold values from -6 to 6
- decay_codes: int32 [4096, 64], P('ctx', 'head'), may hold values from 1 to 8192
- decay_rates: float32 [64], P('head'), may hold values from 2.9296875e-05 to 0.03
- skip_gain: float32 [64], P('head'), may hold values from 0.5 to 2
- norm_gain: float32 [8192], P('head'), may hold values from 0.5 to 1.5
- attend_readout: float32 [8192], P('head'), may hold values from -1.5 to 1.5
- state_readout: float32 [8192], P('head'), may hold values from -0.12 to 0.12
- segment_index: int32 [4096], P('ctx'), may hold values from 0 to 31, never falling along the last dimension, each value on 1 to 256 neighbouring positions
Outputs:
- attended: bfloat16 [4096, 8192], P('ctx', 'head')
- state_mixed: bfloat16 [4096, 8192], P('ctx', 'head')
- segment_values: float32 [32], replicated
All inputs are finite; a program needn't handle non-finite values.
Results may differ from a plain program's by a relative error of at most 0.018.
Values may be sent and summed in bfloat16 or wider, within the bound.
No kernel may reach another device: no remote copies, remote signals or barrier semaphores. Data moves between devices by JAX's collectives and lax.ppermute only.
A program may use at most 64 MiB of HBM per device.

v0:
```python
import math
import jax
import jax.numpy as jnp
from jax import lax
from jax.sharding import PartitionSpec as P

HEADS = 64
KV_HEADS = 8
HEAD_DIM = 128
SCAN_HEADS = 64
SCAN_DIM = 128
STATE = 128
BLOCK = 128
SEG_MEAN = 128
floor_score = -1e30


def prefix(array, axis, combine, identity):
    count, index = (lax.axis_size(axis), lax.axis_index(axis))
    everything = jax.tree.map(
        lambda part, kind: lax.all_gather(part.astype(kind), axis),
        array,
        (jnp.bfloat16, jnp.bfloat16),
    )
    start = jax.tree.map(
        lambda part, zero: jnp.broadcast_to(jnp.asarray(zero, part.dtype), part.shape),
        array,
        identity,
    )

    def turn(k, before):
        reached = k < index
        new = combine(
            before, jax.tree.map(lambda part, own: part[k].astype(own.dtype), everything, array)
        )
        return jax.tree.map(lambda a, b: jnp.where(reached, a, b), new, before)

    return lax.fori_loop(0, count, turn, start)


def absorb_group(inner, keys_piece, values_piece, start, third_request_vector, query_pos):
    rows = keys_piece.shape[0]
    per_head_dimension = third_request_vector.shape[2]
    width = math.gcd(rows, 512)
    scale = per_head_dimension ** (-0.5)

    def one_block(index, state):
        top, total, summed = state
        begin = index * width
        key_block = lax.dynamic_slice_in_dim(keys_piece, begin, width, 0)
        value_block = lax.dynamic_slice_in_dim(values_piece, begin, width, 0)
        scores = (
            jnp.einsum(
                "qhd,kd->qhk", third_request_vector, key_block, preferred_element_type=jnp.float32
            )
            * scale
        )
        key_pos = begin + jnp.arange(width, dtype=jnp.int32)
        allowed = (key_pos[None, :] <= query_pos[:, None])[:, None, :]
        masked = jnp.where(allowed, scores, floor_score)
        new_top = jnp.maximum(top, jnp.max(masked, axis=2))
        weights = jnp.where(allowed, jnp.exp(masked - new_top[:, :, None]), 0.0)
        fade = jnp.exp(top - new_top)
        total = total * fade + jnp.sum(weights, axis=2)
        summed = summed * fade[:, :, None] + jnp.einsum(
            "qhk,kd->qhd",
            weights.astype(jnp.bfloat16),
            value_block,
            preferred_element_type=jnp.float32,
        )
        return (new_top, total, summed)

    def compute(state):
        return lax.fori_loop(0, rows // width, one_block, state)

    def keep(state):
        return state

    needed = jnp.logical_and(start >= 0, start <= jnp.max(query_pos))
    return lax.cond(needed, compute, keep, inner)


def merge_state_pairs(earlier, later):
    return (earlier[0] * later[0], later[0][:, None, None] * earlier[1] + later[1])


def per_device(
    queries,
    key_rows,
    value_rows,
    state_input,
    state_write,
    state_read,
    gate_input,
    decay_codes,
    decay_rates,
    skip_gain,
    norm_gain,
    attend_readout,
    state_readout,
    segment_index,
):
    tokens_here = queries.shape[0]
    heads_here = queries.shape[1] // HEAD_DIM
    n_ctx = lax.axis_size("ctx")
    position = lax.axis_index("ctx")
    first = position * tokens_here
    shared_head = lax.axis_index("head") * heads_here // (HEADS // KV_HEADS)
    key_mine = lax.dynamic_slice_in_dim(key_rows, shared_head * HEAD_DIM, HEAD_DIM, 1)
    value_mine = lax.dynamic_slice_in_dim(value_rows, shared_head * HEAD_DIM, HEAD_DIM, 1)
    scan_here = decay_rates.shape[0]
    blocks = tokens_here // BLOCK
    inputs_four = state_input.reshape(blocks, BLOCK, scan_here, SCAN_DIM)
    write_four = state_write.reshape(blocks, BLOCK, scan_here, STATE)
    read_four = state_read.reshape(blocks, BLOCK, scan_here, STATE)
    log_decay = -decay_rates[None, :] * decay_codes.astype(jnp.float32)
    run = jnp.cumsum(log_decay.reshape(blocks, BLOCK, scan_here), axis=1)
    run_heads = jnp.transpose(run, (0, 2, 1))
    gap = run_heads[:, :, :, None] - run_heads[:, :, None, :]
    places = jnp.arange(BLOCK, dtype=jnp.int32)
    lower = places[:, None] >= places[None, :]
    decay = jnp.where(lower[None, None], jnp.exp(jnp.minimum(gap, 0.0)), 0.0)
    scan_scores = jnp.einsum(
        "bthn,bshn->bhts", read_four, write_four, preferred_element_type=jnp.float32
    )
    mix = (scan_scores * decay).astype(jnp.bfloat16)
    local = jnp.einsum("bhts,bshp->bthp", mix, inputs_four, preferred_element_type=jnp.float32)
    tail = jnp.exp(run[:, -1:, :] - run)
    written = (write_four.astype(jnp.float32) * tail[:, :, :, None]).astype(jnp.bfloat16)
    block_state = jnp.einsum(
        "bshn,bshp->bhnp", written, inputs_four, preferred_element_type=jnp.float32
    )
    block_fade = jnp.exp(run[:, -1, :])

    def carry_step(state, item):
        current, product = state
        fade_now, new_state = item
        return (
            (fade_now[:, None, None] * current + new_state, product * fade_now),
            (current, product),
        )

    start_state = (
        jnp.zeros((scan_here, STATE, SCAN_DIM), jnp.float32),
        jnp.ones((scan_here,), jnp.float32),
    )
    (end_state, total_fade), (entering_local, fade_before) = lax.scan(
        carry_step, start_state, (block_fade, block_state)
    )
    prefix_pair = prefix(
        (total_fade, end_state),
        "ctx",
        merge_state_pairs,
        (jnp.ones_like(total_fade), jnp.zeros_like(end_state)),
    )
    incoming = prefix_pair[1]
    entering = entering_local + fade_before[:, :, None, None] * incoming[None]
    carried = jnp.exp(run)[:, :, :, None] * jnp.einsum(
        "bthn,bhnp->bthp", read_four.astype(jnp.float32), entering, precision=lax.Precision.HIGHEST
    )
    mixed_y = local + carried + skip_gain[None, None, :, None] * inputs_four.astype(jnp.float32)
    gated = mixed_y.reshape(tokens_here, scan_here * SCAN_DIM) * jax.nn.silu(
        gate_input.astype(jnp.float32)
    )
    squares = lax.psum(jnp.sum(gated * gated, axis=1), "head")
    state_mixed = (
        gated * lax.rsqrt(squares / (SCAN_HEADS * SCAN_DIM) + 1e-05)[:, None] * norm_gain[None, :]
    ).astype(jnp.bfloat16)
    groups = (
        (
            queries.reshape(tokens_here, heads_here, HEAD_DIM),
            first + jnp.arange(tokens_here, dtype=jnp.int32),
        ),
    )
    initial = tuple(
        (
            (
                jnp.full((item[0].shape[0], heads_here), floor_score, jnp.float32),
                jnp.zeros((item[0].shape[0], heads_here), jnp.float32),
                jnp.zeros((item[0].shape[0], heads_here, HEAD_DIM), jnp.float32),
            )
            for item in groups
        )
    )
    pieces = (
        lax.all_gather(key_mine, "ctx", axis=0, tiled=True),
        lax.all_gather(value_mine, "ctx", axis=0, tiled=True),
    )
    start = jnp.int32(0)
    inner = tuple(
        (
            absorb_group(
                initial[number], pieces[0], pieces[1], start, groups[number][0], groups[number][1]
            )
            for number in range(len(groups))
        )
    )
    outputs = []
    for state in inner:
        top, total, summed = state
        outputs.append(
            (summed / total[:, :, None])
            .reshape(summed.shape[0], heads_here * HEAD_DIM)
            .astype(jnp.bfloat16)
        )
    attended = outputs[0]
    score = jnp.sum(attended.astype(jnp.float32) * attend_readout[None, :], axis=1)
    score = score + jnp.sum(state_mixed.astype(jnp.float32) * state_readout[None, :], axis=1)
    segment_count = tokens_here * n_ctx // SEG_MEAN
    member = (segment_index[:, None] == jnp.arange(segment_count, dtype=jnp.int32)[None, :]).astype(
        jnp.float32
    )
    partial_sums = jnp.dot(score, member, precision=lax.Precision.HIGHEST)
    counted = jnp.sum(member, axis=0) * (lax.axis_index("head") == 0).astype(jnp.float32)
    sums, counts = lax.psum((partial_sums, counted), ("ctx", "head"))
    return (attended, state_mixed, sums / counts)


def solution(mesh):
    in_specs = (
        P("ctx", "head"),
        P("ctx", None),
        P("ctx", None),
        P("ctx", "head"),
        P("ctx", "head"),
        P("ctx", "head"),
        P("ctx", "head"),
        P("ctx", "head"),
        P("head"),
        P("head"),
        P("head"),
        P("head"),
        P("head"),
        P("ctx"),
    )
    out_specs = (P("ctx", "head"), P("ctx", "head"), P())
    return jax.shard_map(
        per_device, mesh=mesh, in_specs=in_specs, out_specs=out_specs, check_vma=False
    )
```

profile of v0, /device:TPU:1, one launch (start us, length us, event | category | flops | bytes accessed | tf_op | source)
XLA Modules:
  0.0 475.2 jit_solution(627773776391355571)
XLA Ops:
  12.4 1.5 constant_dynamic-slice_fusion.1
  15.5 1.3 dynamic-slice
  17.6 51.5 %all-reduce = bf16[32]{0:T(256)(128)(2,1)S(1)} all-reduce(bf16[32]{0:T(256)(128)(2,1)S(1)} %dynamic-update-slice), channel_id=2, replica_groups=mesh['ctx'=16,'head'=32] {'ctx'}, use_global_device_ids=true, to_apply=%add | all-reduce | flops 32 | bytes 128
  70.3 45.0 %all-gather.10.cloned.1.call-done = bf16[32,128,128]{2,1,0:T(8,128)(2,1)} async-done(((bf16[2,128,128]{2,1,0:T(8,128)(2,1)}), bf16[32,128,128]{2,1,0:T(8,128)(2,1)}) %all-gather.10.cloned.1.call-update) | async-done | bytes 1048592 | tf_op jit(solution)/shard_map/all_gather | solution.py:21
  115.3 15.6 %while.53 = (s32[]{:T(128)}, f32[2,128,128]{2,1,0:T(8,128)S(1)}, s32[]{:T(128)}, bf16[16,2]{1,0:T(8,128)(2,1)S(1)}, bf16[16,2,128,128]{3,2,1,0:T(8,128)(2,1)}) while((s32[]{:T(128)}, f32[2,128,128]{2,1,0:T(8,128)S(1)}, s32[]{:T(128)}, bf16[16,2]{1,0:T(8,128)(2,1)S(1)}, bf16[16,2,128,128]{3,2,1,0:T(8,128)(2,1)}) %tuple.138), condition=%wide.region_11.12_spmd.clone.clone, body=%wide.region_10.11_spmd.clone.sunk.clone | while | flops 163846 | bytes 327797 | solution.py:38
  116.3 0.9 fusion.84
  117.3 0.9 fusion.84
  118.3 0.9 fusion.84
  119.2 0.9 fusion.84
  120.2 0.9 fusion.84
  121.2 0.9 fusion.84
  122.2 0.9 fusion.84
  123.1 0.9 fusion.84
  124.1 0.9 fusion.84
  125.1 0.9 fusion.84
  126.1 0.9 fusion.84
  127.0 0.9 fusion.84
  128.0 0.9 fusion.84
  129.0 0.9 fusion.84
  133.1 141.2 %psum.21 = f32[256]{0:T(256)S(1)} all-reduce(f32[256]{0:T(256)S(1)} %multiply_reduce_fusion.2), channel_id=1, replica_groups=mesh['ctx'=16,'head'=32] {'head'}, use_global_device_ids=true, to_apply=%region_13.14 | all-reduce | flops 256 | bytes 2048 | tf_op jit(solution)/shard_map/psum | solution.py:165
  274.2 45.6 %all-gather.8.cloned.1.call-done = bf16[4096,128]{1,0:T(8,128)(2,1)} async-done(((bf16[256,128]{1,0:T(8,128)(2,1)}), bf16[4096,128]{1,0:T(8,128)(2,1)}) %all-gather.8.cloned.1.call-update) | async-done | bytes 1048592 | tf_op jit(solution)/shard_map/all_gather | solution.py:187
  319.9 40.2 %conditional.1 = (f32[256,2]{0,1:T(2,128)}, f32[256,2,128]{2,0,1:T(8,128)}) conditional(s32[]{:T(128)} %convert_element_type.82, () %tuple.48, (bf16[256,256]{1,0:T(8,128)(2,1)S(1)}, s32[256]{0:T(256)S(1)}, bf16[4096,128]{1,0:T(8,128)(2,1)}, bf16[4096,128]{1,0:T(8,128)(2,1)}) %tuple.137), branch_computations={%region_1.2_spmd, %region_2.7_spmd} | conditional | flops 136907776 | bytes 5149947 | solution.py:80
  320.1 40.0 %while.51 = (s32[]{:T(128)}, f32[256,2]{0,1:T(2,128)S(1)}, f32[256,2]{0,1:T(2,128)}, f32[256,2,128]{2,0,1:T(8,128)}, s32[256]{0:T(256)S(1)}, /*index=5*/bf16[409...) while((s32[]{:T(128)}, f32[256,2]{0,1:T(2,128)S(1)}, ...), condition=%wide.region_6.6_spmd.clone.clone, body=%wide.region_3.5_spmd.clone.sunk.clone | while | flops 136907776 | bytes 4625571 | solution.py:74
  320.3 1.2 fusion.79
  322.4 2.1 convolution_add_fusion.3
  324.6 1.2 fusion.79
  326.1 1.3 fusion.82
  327.3 2.2 convolution_add_fusion.3
  329.7 1.2 fusion.79
  331.1 1.3 fusion.82
  332.4 2.2 convolution_add_fusion.3
  334.8 1.2 fusion.79
  336.2 1.3 fusion.82
  337.5 2.2 convolution_add_fusion.3
  339.9 1.2 fusion.79
  341.3 1.3 fusion.82
  342.6 2.2 convolution_add_fusion.3
  345.0 1.2 fusion.79
  346.4 1.3 fusion.82
  347.7 2.2 convolution_add_fusion.3
  350.1 1.2 fusion.79
  351.5 1.3 fusion.82
  352.8 2.2 convolution_add_fusion.3
  355.1 1.2 fusion.79
  356.6 1.3 fusion.82
  357.9 2.2 convolution_add_fusion.3
  360.8 1.2 multiply_reduce_fusion.1
  363.6 104.5 %all-reduce.1 = (f32[32]{0:T(128)S(1)}, f32[32]{0:T(128)S(1)}) all-reduce(f32[32]{0:T(128)S(1)} %convolution_bitcast_fusion.2, f32[32]{0:T(128)S(1)} %broadcast_multiply_fusion), channel_id=1, replica_groups=mesh['ctx'=16,'head'=32] {'ctx','head'}, use_global_device_ids=true, to_apply=%region_16.17 | all-reduce | flops 64 | bytes 512 | tf_op jit(solution)/shard_map/psum | solution.py:215
  (147 shorter events, 18.5 us)
Async XLA Ops:
  7.2 4.5 copy-start
  7.2 108.1 %all-gather.10.cloned.1.call-start = ((), (), s32[]{:S(2)}) async-start(), calls=%async_computation.2 | async-start | bytes 1114112 | tf_op jit(solution)/shard_map/all_gather | solution.py:21
  7.2 0.7 copy-start.12
  7.3 0.7 copy-start.6
  8.4 0.9 copy-start.2
  9.4 0.9 copy-start.3
  11.6 262.6 %all-gather.6.cloned.1.call-start = ((), (), s32[]{:S(2)}) async-start(), calls=%async_computation | async-start | bytes 1114112 | tf_op jit(solution)/shard_map/all_gather | solution.py:186
  12.3 307.5 %all-gather.8.cloned.1.call-start = ((), (), s32[]{:S(2)}) async-start(), calls=%async_computation.1 | async-start | bytes 1114112 | tf_op jit(solution)/shard_map/all_gather | solution.py:187
  13.9 1.5 copy-start.4
  69.2 0.7 copy-start.11
  130.9 0.7 copy-start.10
  132.0 0.9 copy-start.1
  132.9 187.0 %copy-start.5 = (bf16[256,256]{1,0:T(8,128)(2,1)S(1)}, bf16[256,256]{1,0:T(8,128)(2,1)}, u32[]{:S(2)}) copy-start(bf16[256,256]{1,0:T(8,128)(2,1)} %param.22) | copy-start | bytes 393220
  360.1 0.7 copy-start.7
  360.8 1.2 copy-start.8
  360.8 1.2 copy-start.9
Sparse Core Ops, SparseCore 0:
  11.7 103.5 all-gather.9
  118.0 99.8 all-gather.5
  220.6 99.2 all-gather.7
where the time goes:
time: 477 us; the launch traced here: 475 us
  blocking collectives  297 us (62%)
  waiting for transfers between devices  90.7 us (19%)
  other arithmetic  32.4 us (7%)
  matrix products  28.1 us (6%)
  between operations  15.3 us (3%)
  local copies, waits for them, and re-layouts  10.5 us (2%)
    psum x1, blocking collectives, per_device(): squares = lax.psum(jnp.sum(gated * gated, axis=1), 'head')  141 us
    psum x1, blocking collectives, per_device(): sums, counts = lax.psum((partial_sums, counted), ('ctx', 'head'))  105 us
    unnamed x1, blocking collectives  51.5 us
    all_gather x1, waiting for transfers between devices, per_device(): lax.all_gather(value_mine, 'ctx', axis=0, tiled=True)  45.6 us
    all_gather x1, waiting for transfers between devices, prefix(): lax.all_gather(part.astype(kind), axis)  45 us
    dot_general x8, matrix products, one_block(): jnp.einsum('qhk,kd->qhd', weights.astype(jnp.bfloat16), value_block, pref...  17.4 us
    select_n x16, other arithmetic, turn(): return jax.tree.map(lambda a, b: jnp.where(reached, a, b), new, before)  14.9 us
    dot_general x8, matrix products, one_block(): jnp.einsum('qhd,kd->qhk', third_request_vector, key_block, preferred_elem...  9.77 us
  transfers between devices with their start and end apart: 3, of which 2 were waited for; matrix products, arithmetic and copies ran while one was open for 4% of the time, Pallas kernels for 0%

commit v1 on v0

--- a/solution.py
+++ b/solution.py
@@ -182,10 +182,13 @@
             for item in groups
         )
     )
-    pieces = (
-        lax.all_gather(key_mine, "ctx", axis=0, tiled=True),
-        lax.all_gather(value_mine, "ctx", axis=0, tiled=True),
-    )
+
+    def wait_runs(base_x, dev_axis):
+        low = jnp.stack(tuple((base_x for _ in range(jax.lax.psum(1, dev_axis)))), axis=0)
+        state_next = jax.lax.all_to_all(low, dev_axis, 0, 0)
+        return jnp.concatenate(state_next, 0)
+
+    pieces = (lax.all_gather(key_mine, "ctx", axis=0, tiled=True), wait_runs(value_mine, "ctx"))
     start = jnp.int32(0)
     inner = tuple(
         (

time: 477 us -> 445 us (0.933)
  waiting for transfers between devices: 90.7 us -> 22.1 us
  blocking collectives: 297 us -> 320 us
  starting transfers between devices: 0.12 us -> 14.1 us
    all_gather x1 -> x0, waiting for transfers between devices: 45.6 us -> none  [per_device(): lax.all_gather(value_mine, 'ctx', axis=0, tiled=True)]
    all_gather x1, waiting for transfers between devices: 45 us -> 22 us  [prefix(): lax.all_gather(part.astype(kind), axis)]
    all_to_all x0 -> x1, starting transfers between devices: none -> 14 us  [wait_runs(): state_next = jax.lax.all_to_all(low, dev_axis, 0, 0)]
    psum x1, blocking collectives: 105 us -> 118 us  [per_device(): sums, counts = lax.psum((partial_sums, counted), ('ctx', 'head'))]
    unnamed x1, blocking collectives: 51.5 us -> 61.8 us
  transfers between devices with their start and end apart: 3 -> 3, of which waited for: 2 -> 1; matrix products, arithmetic and copies ran while one was open for 4% -> 5% of each run, Pallas kernels for 0% -> 0%
where the time goes in v1:
time: 445 us; the launch traced here: 443 us
  blocking collectives  320 us (72%)
  other arithmetic  32.3 us (7%)
  matrix products  26.5 us (6%)
  waiting for transfers between devices  22.1 us (5%)
  between operations  15.5 us (3%)
  starting transfers between devices  14.1 us (3%)
  local copies, waits for them, and re-layouts  12 us (3%)
    psum x1, blocking collectives, per_device(): squares = lax.psum(jnp.sum(gated * gated, axis=1), 'head')  141 us
    psum x1, blocking collectives, per_device(): sums, counts = lax.psum((partial_sums, counted), ('ctx', 'head'))  118 us
    unnamed x1, blocking collectives  61.8 us
    all_gather x1, waiting for transfers between devices, prefix(): lax.all_gather(part.astype(kind), axis)  22 us
    dot_general x8, matrix products, one_block(): jnp.einsum('qhk,kd->qhd', weights.astype(jnp.bfloat16), value_block, pref...  15.7 us
    select_n x16, other arithmetic, turn(): return jax.tree.map(lambda a, b: jnp.where(reached, a, b), new, before)  14.9 us
    all_to_all x1, starting transfers between devices, wait_runs(): state_next = jax.lax.all_to_all(low, dev_axis, 0, 0)  14 us
    dot_general x8, matrix products, one_block(): jnp.einsum('qhd,kd->qhk', third_request_vector, key_block, preferred_elem...  9.78 us
  transfers between devices with their start and end apart: 3, of which 1 were waited for; matrix products, arithmetic and copies ran while one was open for 5% of the time, Pallas kernels for 0%

profile of v1, /device:TPU:1, one launch (start us, length us, event | category | flops | bytes accessed | tf_op | source)
XLA Modules:
  0.0 443.2 jit_solution(17581228373003950468)
XLA Ops:
  11.7 1.2 stack.2
  12.9 14.0 %all-to-all-start = ((bf16[16,256,128]{2,1,0:T(8,128)(2,1)}), bf16[16,256,128]{2,1,0:T(8,128)(2,1)S(1)}, u32[]{:S(2)}, u32[]{:S(2)}) async-start(bf16[16,256,128]{2,1,0:T(8,128)(2,1)} %stack.2), calls=%async_computation | async-start | bytes 2097152 | tf_op jit(solution)/shard_map/all_to_all | solution.py:188
  27.0 1.5 constant_dynamic-slice_fusion.1
  30.0 1.3 dynamic-slice
  32.1 61.8 %all-reduce = bf16[32]{0:T(256)(128)(2,1)S(1)} all-reduce(bf16[32]{0:T(256)(128)(2,1)S(1)} %dynamic-update-slice), channel_id=2, replica_groups=mesh['ctx'=16,'head'=32] {'ctx'}, use_global_device_ids=true, to_apply=%add | all-reduce | flops 32 | bytes 128
  95.1 22.0 %all-gather.7.cloned.1.call-done = bf16[32,128,128]{2,1,0:T(8,128)(2,1)} async-done(((bf16[2,128,128]{2,1,0:T(8,128)(2,1)}), bf16[32,128,128]{2,1,0:T(8,128)(2,1)}) %all-gather.7.cloned.1.call-update) | async-done | bytes 1048592 | tf_op jit(solution)/shard_map/all_gather | solution.py:21
  117.1 15.6 %while.53 = (s32[]{:T(128)}, f32[2,128,128]{2,1,0:T(8,128)S(1)}, s32[]{:T(128)}, bf16[16,2]{1,0:T(8,128)(2,1)S(1)}, bf16[16,2,128,128]{3,2,1,0:T(8,128)(2,1)}) while((s32[]{:T(128)}, f32[2,128,128]{2,1,0:T(8,128)S(1)}, s32[]{:T(128)}, bf16[16,2]{1,0:T(8,128)(2,1)S(1)}, bf16[16,2,128,128]{3,2,1,0:T(8,128)(2,1)}) %tuple.137), condition=%wide.region_11.12_spmd.clone.clone, body=%wide.region_10.11_spmd.clone.sunk.clone | while | flops 163846 | bytes 327797 | solution.py:38
  118.1 0.9 fusion.84
  119.1 0.9 fusion.84
  120.1 0.9 fusion.84
  121.0 0.9 fusion.84
  122.0 0.9 fusion.84
  123.0 0.9 fusion.84
  124.0 0.9 fusion.84
  124.9 0.9 fusion.84
  125.9 0.9 fusion.84
  126.9 0.9 fusion.84
  127.9 0.9 fusion.84
  128.8 0.9 fusion.84
  130.8 0.9 fusion.84
  134.8 140.6 %psum.21 = f32[256]{0:T(256)S(1)} all-reduce(f32[256]{0:T(256)S(1)} %multiply_reduce_fusion.2), channel_id=1, replica_groups=mesh['ctx'=16,'head'=32] {'head'}, use_global_device_ids=true, to_apply=%region_13.14 | all-reduce | flops 256 | bytes 2048 | tf_op jit(solution)/shard_map/psum | solution.py:165
  277.0 38.6 %conditional.1 = (f32[256,2]{0,1:T(2,128)}, f32[256,2,128]{2,0,1:T(8,128)}) conditional(s32[]{:T(128)} %convert_element_type.82, () %tuple.48, (bf16[16,256,128]{2,1,0:T(8,128)(2,1)S(1)}, bf16[256,256]{1,0:T(8,128)(2,1)S(1)}, s32[256]{0:T(256)S(1)}, bf16[4096,128]{1,0:T(8,128)(2,1)}) %tuple.136), branch_computations={%region_1.2_spmd, %region_2.7_spmd} | conditional | flops 136907776 | bytes 5149947 | solution.py:80
  277.3 38.3 %while.51 = (s32[]{:T(128)}, f32[256,2]{0,1:T(2,128)S(1)}, f32[256,2]{0,1:T(2,128)}, f32[256,2,128]{2,0,1:T(8,128)}, s32[256]{0:T(256)S(1)}, /*index=5*/bf16[409...) while((s32[]{:T(128)}, f32[256,2]{0,1:T(2,128)S(1)}, ...), condition=%wide.region_6.6_spmd.clone.clone, body=%wide.region_3.5_spmd.clone.sunk.clone | while | flops 136907776 | bytes 4625571 | solution.py:74
  277.4 1.2 fusion.79
  279.5 1.1 convolution_add_fusion.3
  280.8 1.2 fusion.79
  282.3 1.3 fusion.82
  283.6 2.1 convolution_add_fusion.3
  285.8 1.2 fusion.79
  287.3 1.3 fusion.82
  288.5 2.1 convolution_add_fusion.3
  290.8 1.2 fusion.79
  292.3 1.3 fusion.82
  293.5 2.1 convolution_add_fusion.3
  295.8 1.2 fusion.79
  297.3 1.3 fusion.82
  298.5 2.1 convolution_add_fusion.3
  300.8 1.2 fusion.79
  302.2 1.3 fusion.82
  303.5 2.1 convolution_add_fusion.3
  305.8 1.2 fusion.79
  307.2 1.3 fusion.82
  308.5 2.1 convolution_add_fusion.3
  310.8 1.2 fusion.79
  312.2 1.3 fusion.82
  313.5 2.1 convolution_add_fusion.3
  316.3 1.2 multiply_reduce_fusion.1
  318.3 117.6 %all-reduce.1 = (f32[32]{0:T(128)S(1)}, f32[32]{0:T(128)S(1)}) all-reduce(f32[32]{0:T(128)S(1)} %convolution_bitcast_fusion.2, f32[32]{0:T(128)S(1)} %broadcast_multiply_fusion), channel_id=1, replica_groups=mesh['ctx'=16,'head'=32] {'ctx','head'}, use_global_device_ids=true, to_apply=%region_16.17 | all-reduce | flops 64 | bytes 512 | tf_op jit(solution)/shard_map/psum | solution.py:218
  (147 shorter events, 19.5 us)
Async XLA Ops:
  7.2 4.5 %copy-start = (bf16[256,1024]{1,0:T(8,128)(2,1)S(1)}, bf16[256,1024]{1,0:T(8,128)(2,1)}, u32[]{:S(2)}) copy-start(bf16[256,1024]{1,0:T(8,128)(2,1)} %param.24) | copy-start | bytes 1572868
  7.2 110.0 %all-gather.7.cloned.1.call-start = ((), (), s32[]{:S(2)}) async-start(), calls=%async_computation.2 | async-start | bytes 1114112 | tf_op jit(solution)/shard_map/all_gather | solution.py:21
  7.2 0.7 copy-start.12
  7.3 0.7 copy-start.6
  8.4 0.9 copy-start.2
  9.4 0.9 copy-start.3
  12.9 264.0 %all-to-all-start = ((bf16[16,256,128]{2,1,0:T(8,128)(2,1)}), bf16[16,256,128]{2,1,0:T(8,128)(2,1)S(1)}, u32[]{:S(2)}, u32[]{:S(2)}) async-start(bf16[16,256,128]{2,1,0:T(8,128)(2,1)} %stack.2), calls=%async_computation | async-start | bytes 2097152 | tf_op jit(solution)/shard_map/all_to_all | solution.py:188
  26.9 249.9 %all-gather.5.cloned.1.call-start = ((), (), s32[]{:S(2)}) async-start(), calls=%async_computation.1 | async-start | bytes 1114112 | tf_op jit(solution)/shard_map/all_gather | solution.py:191
  28.5 1.4 copy-start.4
  94.0 0.7 copy-start.11
  132.7 0.7 copy-start.10
  133.8 0.9 copy-start.1
  275.4 0.7 copy-start.7
  275.4 0.7 copy-start.8
  276.1 0.9 copy-start.5
  315.6 0.7 copy-start.9
Sparse Core Ops, SparseCore 0:
  11.7 105.3 all-gather.6
  119.8 99.0 all-gather.4
